TPU v7x, 32 devices: a whole 2x2x4 slice. The times are simulated.
32 devices in a mesh: slab: 8 (over y, x, core), field: 4 (over z).
Axes of the slice: x: 2, y: 2, z: 4, core: 2. Of those that a mesh axis runs over, the one named last changes fastest.
Arguments:
- snaps: bfloat16 [4, 16, 3, 32, 2048], P('field', 'slab'), may hold values from -6 to 6
- writer_map: int32 [64], replicated, may hold values from 0 to 63, each once
- omega: int32 [64, 64], replicated, may hold values from -3 to 3
- face_level: int32 [32], replicated, may hold values from 0 to 11
Outputs:
- sketch_rows: float32 [4, 16, 64], P('field')
- core: float32 [64, 64], replicated
All inputs are finite; a program needn't handle non-finite values.
Results may differ from a plain program's by a relative error of at most 0.00035.
Values may be sent and summed in bfloat16 or wider, within the bound.
A program may use at most 128 MiB of HBM per device.

v0:
```python
import jax
import jax.numpy as jnp
from jax import lax
from jax.sharding import PartitionSpec as P


def from_behind(block, axis, distance):
    devices = range(lax.axis_size(axis))
    route = [(i - distance, i) for i in devices if i - distance in devices]
    return lax.ppermute(block, axis, route)


def body(snaps, writer_map, omega, face_level):
    field_count = lax.axis_size("field")
    slab_at = lax.axis_index("slab")
    field_at = lax.axis_index("field")
    sketch_cols = omega.shape[1]
    total_snaps = omega.shape[0]
    total_planes = face_level.shape[0]
    group_rows = total_snaps // field_count
    columns = jnp.arange(total_snaps, dtype=jnp.int32)
    onehot = (writer_map[:, None] == columns[None, :]).astype(jnp.bfloat16)
    test_all = jnp.dot(
        onehot, omega.astype(jnp.bfloat16), preferred_element_type=jnp.float32
    ).astype(jnp.bfloat16)
    local = lax.all_to_all(snaps, "slab", split_axis=3, concat_axis=1, tiled=True)
    comps = local.shape[2]
    planes_dev = local.shape[3]
    cells = local.shape[4]
    features = comps * planes_dev * cells
    test_own = lax.dynamic_slice_in_dim(test_all, field_at * group_rows, group_rows, 0)
    flat = local.reshape(group_rows, features)
    partial_z = jnp.dot(test_own.T, flat, preferred_element_type=jnp.float32)
    sketched = lax.psum(partial_z.astype(jnp.bfloat16), "field").astype(jnp.float32)
    sketched = sketched.reshape(sketch_cols, comps, planes_dev, cells)
    spacing = 0.5 * jnp.power(jnp.float32(1.12), face_level.astype(jnp.float32))
    first_plane = slab_at * planes_dev
    weight = lax.dynamic_slice_in_dim(spacing, first_plane, planes_dev, 0).reshape(
        1, 1, planes_dev, 1
    )
    coupling = lax.dynamic_slice_in_dim(1.0 / spacing, first_plane, planes_dev, 0).reshape(
        1, 1, planes_dev, 1
    )
    scale = 1.0 / (comps * total_planes * cells)
    lower = from_behind(
        sketched[:, :, -1:].astype(jnp.bfloat16), ("slab", "field"), field_count
    ).astype(jnp.float32)
    below = jnp.concatenate([lower, sketched[:, :, :-1]], axis=2)
    flux = coupling * (sketched - below)
    upper = from_behind(
        flux[:, :, :1].astype(jnp.bfloat16), ("slab", "field"), -field_count
    ).astype(jnp.float32)
    above = jnp.concatenate([flux[:, :, 1:], upper], axis=2)
    applied = (
        ((weight * sketched + flux - above) * scale)
        .astype(jnp.bfloat16)
        .reshape(sketch_cols, features)
    )
    partial_rows = lax.dot_general(
        flat, applied, (((1,), (1,)), ((), ())), preferred_element_type=jnp.float32
    )
    blocks = (jnp.arange(field_count, dtype=jnp.int32) == field_at).astype(jnp.float32)
    stored_rows = (blocks[:, None, None] * partial_rows[None, :, :]).reshape(
        total_snaps, sketch_cols
    )
    rows = lax.psum(stored_rows, ("slab", "field"))
    core = (
        jnp.dot(test_all.astype(jnp.float32).T, rows, precision=lax.Precision.HIGHEST) / total_snaps
    )
    own_rows = lax.dynamic_slice_in_dim(rows, field_at * group_rows, group_rows, 0)
    return (own_rows.reshape(1, group_rows, sketch_cols), core)


def solution(mesh):
    in_specs = (P("field", "slab", None, None, None), P(), P(), P())
    out_specs = (P("field", None, None), P())
    return jax.shard_map(body, mesh=mesh, in_specs=in_specs, out_specs=out_specs, check_vma=False)
```

profile of v0, /device:TPU:0, one launch (start us, length us, event | category | flops | bytes accessed | tf_op | source)
XLA Modules:
  0.0 285.8 jit_solution(11686878091657337957)
XLA Ops:
  7.2 2.8 copy.7
  10.0 5.2 %all-to-all-start = ((bf16[1,2,3,32,2048]{4,2,1,0,3:T(4,128)(2,1)}), bf16[1,2,3,32,2048]{4,2,1,0,3:T(4,128)(2,1)S(1)}, u32[]{:S(2)}, u32[]{:S(2)}) async-start(bf16[1,2,3,32,2048]{4,2,1,0,3:T(4,128)(2,1)} %copy.7), calls=%async_computation | async-start | bytes 2097152 | tf_op jit(solution)/shard_map/all_to_all | solution.py:26
  15.2 1.0 convolution_convert_fusion.1
  16.2 14.4 %all-to-all-done = bf16[1,2,3,32,2048]{4,2,1,0,3:T(4,128)(2,1)S(1)} async-done(((bf16[1,2,3,32,2048]{4,2,1,0,3:T(4,128)(2,1)}), bf16[1,2,3,32,2048]{4,2,1,0,3:T(4,128)(2,1)S(1)}, u32[]{:S(2)}, u32[]{:S(2)}) %all-to-all-start) | async-done | bytes 786464 | tf_op jit(solution)/shard_map/all_to_all | solution.py:26
  30.5 0.9 copy.18
  31.5 0.6 reshape.33
  32.1 2.7 convolution_convert_fusion
  34.8 120.6 %all-reduce.2.cloned.1.call-done = bf16[64,24576]{1,0:T(8,128)(2,1)} async-done(((bf16[64,24576]{1,0:T(8,128)(2,1)}), bf16[64,24576]{1,0:T(8,128)(2,1)}) %all-reduce.2.cloned.1.call-update) | async-done | bytes 3145744 | tf_op jit(solution)/shard_map/psum | solution.py:34
  155.4 7.9 %reshape.34 = f32[64,3,4,2048]{3,2,1,0:T(4,128)} reshape(bf16[64,24576]{1,0:T(8,128)(2,1)} %all-reduce.2.cloned.1.call-done) | data formatting | bytes 9437184 | tf_op jit(solution)/shard_map/reshape | solution.py:35
  163.3 4.5 %slice.25 = bf16[64,3,1,2048]{3,2,1,0:T(2,128)(2,1)S(1)} slice(f32[64,3,4,2048]{3,2,1,0:T(4,128)} %reshape.34), slice={[0:64], [0:3], [3:4], [0:2048]} | slice | bytes 1572864 | tf_op jit(solution)/shard_map/slice | solution.py:46
  167.8 0.5 copy.20
  168.2 1.9 collective-permute-start
  170.3 2.3 slice-done.2
  172.6 2.7 copy.19
  175.4 0.2 convert_element_type.42
  175.6 5.9 %pad_maximum_fusion = (f32[64,3,4,2048]{3,0,2,1:T(8,128)}, f32[64,3,4,2048]{3,0,2,1:T(8,128)S(1)}) fusion(f32[64,3,3,2048]{3,0,2,1:T(8,128)S(1)} %copy.19, f32[64,3,1,2048]{3,0,2,1:T(8,128)S(1)} %convert_element_type.42, f32[64,3,4,2048]{3,2,1,0:T(4,128)S(1)} %bitcast.21, f32[4]{0:T(128)S(1)} %dynamic_slice.14), kind=kLoop, calls=%fused_computation.1 | loop fusion | flops 4718592 | bytes 25165840 | tf_op jit(solution)/shard_map/concatenate | solution.py:48
  181.5 2.8 copy-done
  184.3 0.1 slice.24
  184.4 1.3 collective-permute-start.1
  185.9 0.1 broadcast_bitcast_fusion.1
  186.1 0.1 mul.71
  186.2 5.1 %slice.20 = f32[64,3,3,2048]{3,0,2,1:T(8,128)} slice(f32[64,3,4,2048]{3,0,2,1:T(8,128)} %copy-done), slice={[0:64], [0:3], [1:4], [0:2048]} | slice | bytes 9437184 | tf_op jit(solution)/shard_map/slice | solution.py:53
  191.3 6.7 %copy.11 = f32[64,3,4,2048]{3,2,1,0:T(4,128)} copy(f32[64,3,4,2048]{3,0,2,1:T(8,128)S(1)} %bitcast.23) | data formatting | bytes 12582912 | tf_op jit(solution)/shard_map/concatenate | solution.py:48
  198.0 8.0 %concatenate.11 = f32[64,24576]{1,0:T(8,128)} reshape(f32[64,3,4,2048]{3,2,1,0:T(4,128)} %copy.11) | data formatting | bytes 12582912 | tf_op jit(solution)/shard_map/concatenate | solution.py:48
  206.0 1.3 convert_element_type.43
  207.3 2.8 pad_maximum_fusion.1
  210.1 6.6 %copy.13 = f32[64,3,4,2048]{3,2,1,0:T(4,128)} copy(f32[64,3,4,2048]{3,0,2,1:T(8,128)S(1)} %pad_maximum_fusion.1) | data formatting | bytes 12582912 | tf_op jit(solution)/shard_map/concatenate | solution.py:53
  216.7 8.1 %concatenate.13 = f32[64,24576]{1,0:T(8,128)} reshape(f32[64,3,4,2048]{3,2,1,0:T(4,128)} %copy.13) | data formatting | bytes 12582912 | tf_op jit(solution)/shard_map/concatenate | solution.py:53
  224.8 6.4 %fusion.2 = f32[16,64]{1,0:T(8,128)S(1)} fusion(bf16[16,24576]{1,0:T(8,128)(2,1)} %copy-done.2, f32[64,24576]{1,0:T(8,128)} %concatenate.13, f32[64,24576]{1,0:T(8,128)} %concatenate.11, f32[24576]{0:T(1024)S(1)} %bitcast.26, f32[24576]{0:T(1024)S(1)} %bitcast.27, bf16[64,24576]{1,0:T(8,128)(2,1)S(1)} %copy-done.1), kind=kOutput, calls=%fused_computation.11 | convolution fusion | flops 62914560 | bytes 16715776 | tf_op jit(solution)/shard_map/dot_general | solution.py:59
  231.3 46.2 %psum.15 = f32[64,64]{1,0:T(8,128)S(1)} all-reduce(f32[64,64]{1,0:T(8,128)S(1)} %bitcast_multiply_fusion), channel_id=1, replica_groups=mesh['slab'=8,'field'=4] {'slab','field'}, use_global_device_ids=true, to_apply=%region_1.0 | all-reduce | flops 4096 | bytes 32768 | tf_op jit(solution)/shard_map/psum | solution.py:66
  277.5 0.8 convolution_multiply_fusion
  278.3 0.6 dynamic-slice_bitcast_fusion
  (31 shorter events, 0.5 us)
Async XLA Ops:
  10.0 20.6 %all-to-all-start = ((bf16[1,2,3,32,2048]{4,2,1,0,3:T(4,128)(2,1)}), bf16[1,2,3,32,2048]{4,2,1,0,3:T(4,128)(2,1)S(1)}, u32[]{:S(2)}, u32[]{:S(2)}) async-start(bf16[1,2,3,32,2048]{4,2,1,0,3:T(4,128)(2,1)} %copy.7), calls=%async_computation | async-start | bytes 2097152 | tf_op jit(solution)/shard_map/all_to_all | solution.py:26
  15.1 140.3 %all-reduce.2.cloned.1.call-start = ((), (), s32[]{:S(2)}) async-start(), calls=%async_computation.1 | async-start | bytes 6291456 | tf_op jit(solution)/shard_map/psum | solution.py:34
  32.1 131.2 %copy-start.2 = (bf16[16,24576]{1,0:T(8,128)(2,1)}, bf16[16,24576]{1,0:T(8,128)(2,1)S(1)}, u32[]{:S(2)}) copy-start(bf16[16,24576]{1,0:T(8,128)(2,1)S(1)} %reshape.33) | copy-start | bytes 2359300
  34.8 135.4 %copy-start.3 = (s32[32]{0:T(128)S(1)}, s32[32]{0:T(128)}, u32[]{:S(2)}) copy-start(s32[32]{0:T(128)} %param.7) | copy-start | bytes 388
  168.2 7.1 %collective-permute-start = (bf16[64,3,1,2048]{3,0,2,1:T(8,128)(2,1)S(1)}, bf16[64,3,1,2048]{3,0,2,1:T(8,128)(2,1)S(1)}, u32[]{:S(2)}, u32[]{:S(2)}) collective-permute-start(bf16[64,3,1,2048]{3,0,2,1:T(8,128)(2,1)S(1)} %copy.20), channel_id=1, source_target_pairs={{0,4},{1,5},{2,6},{3,7},{4,8},{5,9},{6,10},{7,11},{8,12},{9,13},{1... | collective-permute-start | bytes 2359304 | tf_op jit(solution)/shard_map/ppermute | solution.py:10
  170.3 2.3 slice-start.2
  170.3 5.3 %slice-start = ((s8[6291456]{0:T(1024)(128)(4,1)}), s8[4194304]{0:T(1024)(128)(4,1)S(1)}, s32[]{:S(2)}) async-start(s8[6291456]{0:T(1024)(128)(4,1)} %bitcast.20), calls=%async_computation.2 | async-start | bytes 8388608
  172.6 2.9 %slice-start.1 = ((s8[6291456]{0:T(1024)(128)(4,1)}), s8[2097152]{0:T(1024)(128)(4,1)S(1)}, s32[]{:S(2)}) async-start(s8[6291456]{0:T(1024)(128)(4,1)} %bitcast.20), calls=%async_computation.3 | async-start | bytes 4194304
  181.5 2.8 copy-start
  181.5 9.9 %slice-start.3 = ((s8[6291456]{0:T(1024)(128)(4,1)}), s8[2097152]{0:T(1024)(128)(4,1)S(1)}, s32[]{:S(2)}) async-start(s8[6291456]{0:T(1024)(128)(4,1)} %bitcast.22), calls=%async_computation.5 | async-start | bytes 4194304
  184.4 21.6 %collective-permute-start.1 = (bf16[64,3,1,2048]{3,0,2,1:T(8,128)(2,1)S(1)}, bf16[64,3,1,2048]{3,0,2,1:T(8,128)(2,1)}, u32[]{:S(2)}, u32[]{:S(2)}) collective-permute-start(bf16[64,3,1,2048]{3,0,2,1:T(8,128)(2,1)S(1)} %slice.24), channel_id=1, source_target_pairs={{4,0},{5,1},{6,2},{7,3},{8,4},{9,5},{10,6},{11,7},{12,8},{13,9},{1... | collective-permute-start | bytes 2359304 | tf_op jit(solution)/shard_map/ppermute | solution.py:10
  186.2 5.1 %slice-start.4 = ((s8[6291456]{0:T(1024)(128)(4,1)}), s8[4194304]{0:T(1024)(128)(4,1)S(1)}, s32[]{:S(2)}) async-start(s8[6291456]{0:T(1024)(128)(4,1)} %bitcast.22), calls=%async_computation.6 | async-start | bytes 8388608
  216.7 8.1 %copy-start.1 = (bf16[64,24576]{1,0:T(8,128)(2,1)S(1)}, bf16[64,24576]{1,0:T(8,128)(2,1)}, u32[]{:S(2)}) copy-start(bf16[64,24576]{1,0:T(8,128)(2,1)} %all-reduce.2.cloned.1.call-done) | copy-start | bytes 9437188
Sparse Core Ops, SparseCore 0:
  34.9 120.4 all-reduce.1
where the time goes:
time: 286 us
  waiting for transfers between devices  135 us (47%)
  local copies, waits for them, and re-layouts  60.8 us (21%)
  blocking collectives  46.2 us (16%)
  between operations  14.2 us (5%)
  matrix products  10.9 us (4%)
  other arithmetic  10.2 us (4%)
  starting transfers between devices  8.43 us (3%)
    psum x1, waiting for transfers between devices, body(): lax.psum(partial_z.astype(jnp.bfloat16), 'field').astype(jnp.float32)  121 us
    psum x1, blocking collectives, body(): rows = lax.psum(stored_rows, ('slab', 'field'))  46.2 us
    concatenate x2, local copies, waits for them, and re-layouts, body(): above = jnp.concatenate([flux[:, :, 1:], upper], axis=2)  14.7 us
    concatenate x2, local copies, waits for them, and re-layouts, body(): below = jnp.concatenate([lower, sketched[:, :, :-1]], axis=2)  14.6 us
    all_to_all x1, waiting for transfers between devices, body(): lax.all_to_all(snaps, 'slab', split_axis=3, concat_axis=1, tiled=True)  14.4 us
    unnamed x23, local copies, waits for them, and re-layouts  9.04 us
    reshape x1, local copies, waits for them, and re-layouts, body(): sketched = sketched.reshape(sketch_cols, comps, planes_dev, cells)  7.87 us
    dot_general x1, matrix products, body(): lax.dot_general(flat, applied, (((1,), (1,)), ((), ())), preferred_elemen...  6.4 us
  transfers between devices with their start and end apart: 4, of which 2 were waited for; matrix products, arithmetic and copies ran while one was open for 8% of the time, Pallas kernels for 0%

commit v1 on v0

--- a/solution.py
+++ b/solution.py
@@ -2,6 +2,9 @@
 import jax.numpy as jnp
 from jax import lax
 from jax.sharding import PartitionSpec as P
+from jax.lax import psum
+
+end_view = lambda w_in, group_axis, net_axis: psum(psum(w_in, net_axis), axis_name=group_axis)
 
 
 def from_behind(block, axis, distance):
@@ -63,7 +66,7 @@
     stored_rows = (blocks[:, None, None] * partial_rows[None, :, :]).reshape(
         total_snaps, sketch_cols
     )
-    rows = lax.psum(stored_rows, ("slab", "field"))
+    rows = end_view(stored_rows, "field", "slab")
     core = (
         jnp.dot(test_all.astype(jnp.float32).T, rows, precision=lax.Precision.HIGHEST) / total_snaps
     )

time: 286 us -> 290 us (1.014)
  blocking collectives: 46.2 us -> 49.3 us
    psum x1 -> x2, blocking collectives: 46.2 us -> 49.3 us  [the longest x1 32.4 us: psum(w_in, net_axis)]
where the time goes in v1:
time: 290 us; the launch traced here: 289 us
  waiting for transfers between devices  135 us (47%)
  local copies, waits for them, and re-layouts  60.8 us (21%)
  blocking collectives  49.3 us (17%)
  between operations  14.2 us (5%)
  matrix products  10.8 us (4%)
  other arithmetic  10.3 us (4%)
  starting transfers between devices  8.43 us (3%)
    psum x1, waiting for transfers between devices, body(): lax.psum(partial_z.astype(jnp.bfloat16), 'field').astype(jnp.float32)  121 us
    psum x1, blocking collectives, psum(w_in, net_axis)  32.4 us
    psum x1, blocking collectives, psum(psum(w_in, net_axis), axis_name=group_axis)  16.9 us
    concatenate x2, local copies, waits for them, and re-layouts, body(): above = jnp.concatenate([flux[:, :, 1:], upper], axis=2)  14.7 us
    concatenate x2, local copies, waits for them, and re-layouts, body(): below = jnp.concatenate([lower, sketched[:, :, :-1]], axis=2)  14.6 us
    all_to_all x1, waiting for transfers between devices, body(): lax.all_to_all(snaps, 'slab', split_axis=3, concat_axis=1, tiled=True)  14.4 us
    unnamed x23, local copies, waits for them, and re-layouts  9.03 us
    reshape x1, local copies, waits for them, and re-layouts, body(): sketched = sketched.reshape(sketch_cols, comps, planes_dev, cells)  7.86 us
  transfers between devices with their start and end apart: 4, of which 2 were waited for; matrix products, arithmetic and copies ran while one was open for 8% of the time, Pallas kernels for 0%

profile of v1, /device:TPU:0, one launch (start us, length us, event | category | flops | bytes accessed | tf_op | source)
XLA Modules:
  0.0 288.8 jit_solution(5655374758496263184)
XLA Ops:
  7.2 2.8 copy.7
  10.0 5.2 %all-to-all-start = ((bf16[1,2,3,32,2048]{4,2,1,0,3:T(4,128)(2,1)}), bf16[1,2,3,32,2048]{4,2,1,0,3:T(4,128)(2,1)S(1)}, u32[]{:S(2)}, u32[]{:S(2)}) async-start(bf16[1,2,3,32,2048]{4,2,1,0,3:T(4,128)(2,1)} %copy.7), calls=%async_computation | async-start | bytes 2097152 | tf_op jit(solution)/shard_map/all_to_all | solution.py:29
  15.2 1.0 convolution_convert_fusion.1
  16.1 14.4 %all-to-all-done = bf16[1,2,3,32,2048]{4,2,1,0,3:T(4,128)(2,1)S(1)} async-done(((bf16[1,2,3,32,2048]{4,2,1,0,3:T(4,128)(2,1)}), bf16[1,2,3,32,2048]{4,2,1,0,3:T(4,128)(2,1)S(1)}, u32[]{:S(2)}, u32[]{:S(2)}) %all-to-all-start) | async-done | bytes 786464 | tf_op jit(solution)/shard_map/all_to_all | solution.py:29
  30.5 0.9 copy.18
  31.5 0.6 reshape.33
  32.1 2.6 convolution_convert_fusion
  34.7 120.6 %all-reduce.2.cloned.1.call-done = bf16[64,24576]{1,0:T(8,128)(2,1)} async-done(((bf16[64,24576]{1,0:T(8,128)(2,1)}), bf16[64,24576]{1,0:T(8,128)(2,1)}) %all-reduce.2.cloned.1.call-update) | async-done | bytes 3145744 | tf_op jit(solution)/shard_map/psum | solution.py:37
  155.4 7.9 %reshape.34 = f32[64,3,4,2048]{3,2,1,0:T(4,128)} reshape(bf16[64,24576]{1,0:T(8,128)(2,1)} %all-reduce.2.cloned.1.call-done) | data formatting | bytes 9437184 | tf_op jit(solution)/shard_map/reshape | solution.py:38
  163.2 4.5 %slice.25 = bf16[64,3,1,2048]{3,2,1,0:T(2,128)(2,1)S(1)} slice(f32[64,3,4,2048]{3,2,1,0:T(4,128)} %reshape.34), slice={[0:64], [0:3], [3:4], [0:2048]} | slice | bytes 1572864 | tf_op jit(solution)/shard_map/slice | solution.py:49
  167.7 0.5 copy.20
  168.2 1.9 collective-permute-start
  170.2 2.3 slice-done.2
  172.6 2.7 copy.19
  175.3 0.2 convert_element_type.42
  175.5 5.9 %pad_maximum_fusion = (f32[64,3,4,2048]{3,0,2,1:T(8,128)}, f32[64,3,4,2048]{3,0,2,1:T(8,128)S(1)}) fusion(f32[64,3,3,2048]{3,0,2,1:T(8,128)S(1)} %copy.19, f32[64,3,1,2048]{3,0,2,1:T(8,128)S(1)} %convert_element_type.42, f32[64,3,4,2048]{3,2,1,0:T(4,128)S(1)} %bitcast.21, f32[4]{0:T(128)S(1)} %dynamic_slice.14), kind=kLoop, calls=%fused_computation.1 | loop fusion | flops 4718592 | bytes 25165840 | tf_op jit(solution)/shard_map/concatenate | solution.py:51
  181.5 2.8 copy-done
  184.3 0.1 slice.24
  184.4 1.3 collective-permute-start.1
  186.1 0.1 mul.71
  186.2 5.1 %slice.20 = f32[64,3,3,2048]{3,0,2,1:T(8,128)} slice(f32[64,3,4,2048]{3,0,2,1:T(8,128)} %copy-done), slice={[0:64], [0:3], [1:4], [0:2048]} | slice | bytes 9437184 | tf_op jit(solution)/shard_map/slice | solution.py:56
  191.3 6.7 %copy.11 = f32[64,3,4,2048]{3,2,1,0:T(4,128)} copy(f32[64,3,4,2048]{3,0,2,1:T(8,128)S(1)} %bitcast.23) | data formatting | bytes 12582912 | tf_op jit(solution)/shard_map/concatenate | solution.py:51
  198.0 8.0 %concatenate.11 = f32[64,24576]{1,0:T(8,128)} reshape(f32[64,3,4,2048]{3,2,1,0:T(4,128)} %copy.11) | data formatting | bytes 12582912 | tf_op jit(solution)/shard_map/concatenate | solution.py:51
  206.0 1.3 convert_element_type.43
  207.3 2.8 pad_maximum_fusion.1
  210.1 6.6 %copy.13 = f32[64,3,4,2048]{3,2,1,0:T(4,128)} copy(f32[64,3,4,2048]{3,0,2,1:T(8,128)S(1)} %pad_maximum_fusion.1) | data formatting | bytes 12582912 | tf_op jit(solution)/shard_map/concatenate | solution.py:56
  216.7 8.1 %concatenate.13 = f32[64,24576]{1,0:T(8,128)} reshape(f32[64,3,4,2048]{3,2,1,0:T(4,128)} %copy.13) | data formatting | bytes 12582912 | tf_op jit(solution)/shard_map/concatenate | solution.py:56
  224.8 6.4 %fusion.2 = f32[16,64]{1,0:T(8,128)S(1)} fusion(bf16[16,24576]{1,0:T(8,128)(2,1)} %copy-done.2, f32[64,24576]{1,0:T(8,128)} %concatenate.13, f32[64,24576]{1,0:T(8,128)} %concatenate.11, f32[24576]{0:T(1024)S(1)} %bitcast.26, f32[24576]{0:T(1024)S(1)} %bitcast.27, bf16[64,24576]{1,0:T(8,128)(2,1)S(1)} %copy-done.1), kind=kOutput, calls=%fused_computation.11 | convolution fusion | flops 62914560 | bytes 16715776 | tf_op jit(solution)/shard_map/dot_general | solution.py:62
  231.3 32.4 %psum.22 = f32[64,64]{1,0:T(8,128)S(1)} all-reduce(f32[64,64]{1,0:T(8,128)S(1)} %bitcast_multiply_fusion), channel_id=1, replica_groups=mesh['slab'=8,'field'=4] {'slab'}, use_global_device_ids=true, to_apply=%region_1.0 | all-reduce | flops 4096 | bytes 32768 | tf_op jit(solution)/shard_map/psum | solution.py:7
  263.6 16.9 %psum.23 = f32[64,64]{1,0:T(8,128)S(1)} all-reduce(f32[64,64]{1,0:T(8,128)S(1)} %psum.22), channel_id=1, replica_groups=mesh['slab'=8,'field'=4] {'field'}, use_global_device_ids=true, to_apply=%region_2.0 | all-reduce | flops 4096 | bytes 32768 | tf_op jit(solution)/shard_map/psum | solution.py:7
  280.6 0.8 convolution_multiply_fusion
  281.4 0.6 dynamic-slice_bitcast_fusion
  (32 shorter events, 0.6 us)
Async XLA Ops:
  10.0 20.6 %all-to-all-start = ((bf16[1,2,3,32,2048]{4,2,1,0,3:T(4,128)(2,1)}), bf16[1,2,3,32,2048]{4,2,1,0,3:T(4,128)(2,1)S(1)}, u32[]{:S(2)}, u32[]{:S(2)}) async-start(bf16[1,2,3,32,2048]{4,2,1,0,3:T(4,128)(2,1)} %copy.7), calls=%async_computation | async-start | bytes 2097152 | tf_op jit(solution)/shard_map/all_to_all | solution.py:29
  15.1 140.2 %all-reduce.2.cloned.1.call-start = ((), (), s32[]{:S(2)}) async-start(), calls=%async_computation.1 | async-start | bytes 6291456 | tf_op jit(solution)/shard_map/psum | solution.py:37
  32.1 131.2 %copy-start.2 = (bf16[16,24576]{1,0:T(8,128)(2,1)}, bf16[16,24576]{1,0:T(8,128)(2,1)S(1)}, u32[]{:S(2)}) copy-start(bf16[16,24576]{1,0:T(8,128)(2,1)S(1)} %reshape.33) | copy-start | bytes 2359300
  34.7 135.4 %copy-start.3 = (s32[32]{0:T(128)S(1)}, s32[32]{0:T(128)}, u32[]{:S(2)}) copy-start(s32[32]{0:T(128)} %param.7) | copy-start | bytes 388
  168.2 7.1 %collective-permute-start = (bf16[64,3,1,2048]{3,0,2,1:T(8,128)(2,1)S(1)}, bf16[64,3,1,2048]{3,0,2,1:T(8,128)(2,1)S(1)}, u32[]{:S(2)}, u32[]{:S(2)}) collective-permute-start(bf16[64,3,1,2048]{3,0,2,1:T(8,128)(2,1)S(1)} %copy.20), channel_id=1, source_target_pairs={{0,4},{1,5},{2,6},{3,7},{4,8},{5,9},{6,10},{7,11},{8,12},{9,13},{1... | collective-permute-start | bytes 2359304 | tf_op jit(solution)/shard_map/ppermute | solution.py:13
  170.2 2.3 slice-start.2
  170.2 5.3 %slice-start = ((s8[6291456]{0:T(1024)(128)(4,1)}), s8[4194304]{0:T(1024)(128)(4,1)S(1)}, s32[]{:S(2)}) async-start(s8[6291456]{0:T(1024)(128)(4,1)} %bitcast.20), calls=%async_computation.2 | async-start | bytes 8388608
  172.6 2.9 %slice-start.1 = ((s8[6291456]{0:T(1024)(128)(4,1)}), s8[2097152]{0:T(1024)(128)(4,1)S(1)}, s32[]{:S(2)}) async-start(s8[6291456]{0:T(1024)(128)(4,1)} %bitcast.20), calls=%async_computation.3 | async-start | bytes 4194304
  181.5 2.8 copy-start
  181.5 9.9 %slice-start.3 = ((s8[6291456]{0:T(1024)(128)(4,1)}), s8[2097152]{0:T(1024)(128)(4,1)S(1)}, s32[]{:S(2)}) async-start(s8[6291456]{0:T(1024)(128)(4,1)} %bitcast.22), calls=%async_computation.5 | async-start | bytes 4194304
  184.4 21.6 %collective-permute-start.1 = (bf16[64,3,1,2048]{3,0,2,1:T(8,128)(2,1)S(1)}, bf16[64,3,1,2048]{3,0,2,1:T(8,128)(2,1)}, u32[]{:S(2)}, u32[]{:S(2)}) collective-permute-start(bf16[64,3,1,2048]{3,0,2,1:T(8,128)(2,1)S(1)} %slice.24), channel_id=1, source_target_pairs={{4,0},{5,1},{6,2},{7,3},{8,4},{9,5},{10,6},{11,7},{12,8},{13,9},{1... | collective-permute-start | bytes 2359304 | tf_op jit(solution)/shard_map/ppermute | solution.py:13
  186.2 5.2 %slice-start.4 = ((s8[6291456]{0:T(1024)(128)(4,1)}), s8[4194304]{0:T(1024)(128)(4,1)S(1)}, s32[]{:S(2)}) async-start(s8[6291456]{0:T(1024)(128)(4,1)} %bitcast.22), calls=%async_computation.6 | async-start | bytes 8388608
  216.7 8.1 %copy-start.1 = (bf16[64,24576]{1,0:T(8,128)(2,1)S(1)}, bf16[64,24576]{1,0:T(8,128)(2,1)}, u32[]{:S(2)}) copy-start(bf16[64,24576]{1,0:T(8,128)(2,1)} %all-reduce.2.cloned.1.call-done) | copy-start | bytes 9437188
Sparse Core Ops, SparseCore 0:
  34.9 120.4 all-reduce.1
